TPU v7x, 32 devices: a whole 2x2x4 slice. The times are simulated.
32 devices in a mesh: seq: 16 (over z, x, core), head: 2 (over y).
Axes of the slice: x: 2, y: 2, z: 4, core: 2. Of those that a mesh axis runs over, the one named last changes fastest.
Arguments:
- queries: bfloat16 [6144, 4096], P('seq', 'head'), may hold values from -8 to 8
- keys: bfloat16 [6144, 4096], P('seq', 'head'), may hold values from -8 to 8
- values: bfloat16 [6144, 4096], P('seq', 'head'), may hold values from -6 to 6
- target_row: int32 [6144], P('seq'), may hold values from 0 to 6143, as said below
- doc_lengths: int32 [32], replicated, may hold values from 0 to 3072, as said below
Outputs:
- mixed: bfloat16 [6144, 4096], P('seq', 'head')
Inputs may be any that keep to these rules, and one draw needn't show every extreme that they name: `target_row`: A permutation of the rows. The rows of one device go to at most 36 rows of any one device's block of 384 rows in document order, and every device sends exactly 36 rows to some device. `doc_lengths`: they sum to 6144; zero lengths occur; no document crosses a multiple of 3072 rows, and some document fills the rows between two such multiples.
All inputs are finite; a program needn't handle non-finite values.
Results may differ from a plain program's by a relative error of at most 0.0035.
Values may be sent and summed in bfloat16 or wider, within the bound.
No kernel may reach another device: no remote copies, remote signals or barrier semaphores. Data moves between devices by JAX's collectives and lax.ppermute only.
A program may use at most 64 MiB of HBM per device.

v0:
```python
import functools
import math

import jax
import jax.numpy as jnp
from jax import lax
from jax.experimental import pallas as pl
from jax.experimental.pallas import tpu as pltpu
from jax.sharding import PartitionSpec as P

HD = 128
SUB = 16
BASE = 64
NEG = -1e30
EXP2_SCALE = math.log2(math.e) / math.sqrt(HD)
VMEM_LIMIT = 40 * 1024 * 1024
SORT_LIMIT = 60 * 1024 * 1024


def rounded_up(count, multiple):
    return -(-count // multiple) * multiple


def sort_kernel(units, span_rows, cap, total, target_ref, q_ref, k_ref, v_ref, out_ref, onehot, notes):
    rows = q_ref.shape[0]
    lanes = 3 * HD

    @pl.when(pl.program_id(0) == 0)
    def _():
        across = jnp.concatenate([target_ref[n : n + 1, :] for n in range(rows // HD)], axis=1)
        down = jnp.concatenate(
            [
                jnp.transpose(jnp.broadcast_to(target_ref[n : n + 1, :], (HD, HD)))
                for n in range(rows // HD)
            ],
            axis=0,
        )
        down = jnp.concatenate([down] * (rows // HD), axis=1)
        unit = jnp.zeros_like(across)
        for u in range(1, units):
            unit += (across >= u * span_rows).astype(jnp.int32)
        inner = across - unit * span_rows
        before = (down < across) & (down >= unit * span_rows)
        place = jnp.sum(before.astype(jnp.int32), axis=0, keepdims=True)
        slot = jnp.where(place < cap, unit * total + place, -1)
        slots = lax.broadcasted_iota(jnp.int32, (units * total, rows), 0)
        onehot[...] = jnp.where(slots == slot, 1.0, 0.0).astype(jnp.bfloat16)
        crowded = jnp.max(jnp.where(place >= cap, 1.0, 0.0), axis=1, keepdims=True)
        high = inner // BASE
        kind = lax.broadcasted_iota(jnp.int32, (SUB, rows), 0)
        digits = jnp.where(kind == 0, high + 1, jnp.where(kind == 1, inner - high * BASE, 0))
        digits = digits.astype(jnp.float32).astype(jnp.bfloat16)
        spread = lax.broadcasted_iota(jnp.int32, (lanes, rows), 0)
        line = lax.broadcasted_iota(jnp.int32, (total, lanes), 0)
        for u in range(units):
            mine = jnp.where((spread == place) & (unit == u), 1.0, 0.0).astype(jnp.bfloat16)
            along = lax.dot_general(
                digits, mine, (((1,), (1,)), ((), ())), preferred_element_type=jnp.float32
            )
            note = jnp.where(line == total - 3, along[0:1], jnp.where(line == total - 2, along[1:2], 0.0))
            note = jnp.where(line == total - 1, crowded, note)
            notes[u * total : (u + 1) * total, :] = note.astype(jnp.bfloat16)

    for m in range(q_ref.shape[1] // HD):
        cols = slice(m * HD, (m + 1) * HD)
        block = jnp.concatenate([q_ref[:, cols], k_ref[:, cols], v_ref[:, cols]], axis=1)
        sent = jnp.dot(onehot[...], block, preferred_element_type=jnp.float32).astype(jnp.bfloat16)
        out_ref[:, m] = (sent + notes[...]).reshape(units, total, lanes)


def sort_rows(queries, keys, values, target_row, units, span, cap, total, chunk):
    rows = queries.shape[0]
    steps = math.gcd(span, 2)
    count = span // steps
    column = pl.BlockSpec((rows, count * HD), lambda n: (0, chunk * steps + n))
    sent = pl.pallas_call(
        functools.partial(sort_kernel, units, span * rows, cap, total),
        grid=(steps,),
        out_shape=jax.ShapeDtypeStruct((units, span, total, 3 * HD), jnp.bfloat16),
        in_specs=[
            pl.BlockSpec((rows // HD, HD), lambda n: (0, 0)),
            column,
            column,
            column,
        ],
        out_specs=pl.BlockSpec((units, count, total, 3 * HD), lambda n: (0, n, 0, 0)),
        scratch_shapes=[
            pltpu.VMEM((units * total, rows), jnp.bfloat16),
            pltpu.VMEM((units * total, 3 * HD), jnp.bfloat16),
        ],
        compiler_params=pltpu.CompilerParams(vmem_limit_bytes=SORT_LIMIT),
        cost_estimate=pl.CostEstimate(
            flops=2 * units * span * total * rows * 3 * HD,
            bytes_accessed=2 * 3 * HD * span * (rows + units * total),
            transcendentals=0,
        ),
        name="sort_rows",
    )(target_row.reshape(rows // HD, HD), queries, keys, values)
    return sent.reshape(units * span, total, 3 * HD)


def plan_kernel(devices, span, rows, total, win, *refs):
    tail_ref, offset_ref, place_ref, crowded_ref = refs
    tail = tail_ref[...].astype(jnp.float32)
    lines = [tail[n, SUB - 3 :, :] for n in range(devices)]
    high = jnp.concatenate([line[0:1] for line in lines], axis=0)
    low = jnp.concatenate([line[1:2] for line in lines], axis=0)
    crowded = jnp.concatenate([line[2:3] for line in lines], axis=0)
    crowded_ref[...] = jnp.max(jnp.max(crowded, axis=1, keepdims=True), axis=0, keepdims=True).astype(jnp.int32)
    place = jnp.where(high > 0.0, (high - 1.0) * BASE + low, -1.0).astype(jnp.int32)
    per = max(HD // win, 1)
    groups = devices // per
    wide = per * win
    lane = lax.broadcasted_iota(jnp.int32, (groups, wide), 1)
    shifted = {}
    for t in range((total - win) // SUB + 1):
        for e in range(per):
            turn = (e * win - SUB * t) % (3 * HD)
            part = place[e * groups : (e + 1) * groups]
            shifted[t, e] = (pltpu.roll(part, turn, 1) if turn else part)[:, :wide]
    for d in range(span):
        begun = jnp.sum(jnp.where((place >= 0) & (place < d * rows), 1, 0), axis=1, keepdims=True)
        offset = jnp.minimum(begun // SUB * SUB, total - win)
        offset_ref[d] = jnp.broadcast_to(offset, (devices, HD))
        out = jnp.full((groups, wide), -1, jnp.int32)
        for (t, e), part in shifted.items():
            mine = (offset[e * groups : (e + 1) * groups] == SUB * t) & (lane >= e * win) & (lane < (e + 1) * win)
            out = jnp.where(mine, part, out)
        place_ref[d] = out


def plan_rows(received, devices, span, rows, total, win):
    wide = max(HD // win, 1) * win
    groups = devices * win // wide
    last = total // SUB - 1
    offsets, places, crowded = pl.pallas_call(
        functools.partial(plan_kernel, devices, span, rows, total, win),
        grid=(1,),
        out_shape=[
            jax.ShapeDtypeStruct((span, devices, HD), jnp.int32),
            jax.ShapeDtypeStruct((span, groups, wide), jnp.int32),
            jax.ShapeDtypeStruct((1, 1), jnp.int32),
        ],
        in_specs=[pl.BlockSpec((devices, SUB, 3 * HD), lambda n: (0, last, 0))],
        out_specs=[
            pl.BlockSpec((span, devices, HD), lambda n: (0, 0, 0)),
            pl.BlockSpec((span, groups, wide), lambda n: (0, 0, 0)),
            pl.BlockSpec((1, 1), lambda n: (0, 0)),
        ],
        compiler_params=pltpu.CompilerParams(vmem_limit_bytes=VMEM_LIMIT),
        name="plan_rows",
    )(received)
    return offsets[:, :, 0].reshape(-1), places, crowded[0, 0] > 0


def attend_kernel(rows, span, win, block, number_ref, place_ref, first_ref, recv_ref, *refs):
    out_refs = refs[-11 - span : -11]
    q_all, k_all, v_all, windows, begins, top, mixed, scores, weights, fades, totals = refs[-11:]
    devices = recv_ref.shape[0]
    groups, wide = place_ref.shape[1:]
    per = wide // win
    blocks = span * rows // block
    lanes = [slice(n * HD, (n + 1) * HD) for n in range(block // HD)]

    def low_of(i):
        return number_ref[1 + i]

    def high_of(i):
        return number_ref[1 + blocks + i]

    part = min(32, block)

    @pl.when(high_of(blocks - 1) > 0)
    def _():
        for n in range(span * rows // HD):
            begin = jnp.broadcast_to(first_ref[n : n + 1, :], (HD, HD))
            begins[n * HD : (n + 1) * HD, :] = jnp.transpose(begin)

    spot = lax.broadcasted_iota(jnp.int32, (rows, wide), 0)
    for d in range(span):
        here = slice(d * rows, (d + 1) * rows)
        window = windows[d % 2]
        for p in range(groups):
            for e in range(per):
                i = e * groups + p
                offset = pl.multiple_of(number_ref[1 + 2 * blocks + d * devices + i], SUB)
                slot = p * wide + e * win
                window[slot : slot + win, :] = recv_ref[i, pl.ds(offset, win), :]
        onehot = [
            jnp.where(spot == place_ref[d, p : p + 1, :] - d * rows, 1.0, 0.0).astype(jnp.bfloat16)
            for p in range(groups)
        ]
        onehot = jnp.concatenate(onehot, axis=1) if groups > 1 else onehot[0]
        placed = jnp.dot(onehot, window[...], preferred_element_type=jnp.float32)
        scaled = placed[:, :HD] * EXP2_SCALE
        high = scaled.astype(jnp.bfloat16)
        q_all[here, :HD] = high
        q_all[here, HD:] = (scaled - high.astype(jnp.float32)).astype(jnp.bfloat16)
        key = placed[:, HD : 2 * HD].astype(jnp.bfloat16)
        k_all[here, :HD] = key
        k_all[here, HD:] = key
        v_all[here, :HD] = placed[:, 2 * HD :].astype(jnp.bfloat16)

    def starting(index):
        return pl.multiple_of(index * block, block)

    def score(i, j, slot):
        scores[slot][...] = lax.dot_general(
            q_all[pl.ds(starting(i), block), :],
            k_all[pl.ds(starting(j), block), :],
            (((1,), (1,)), ((), ())),
            preferred_element_type=jnp.float32,
        )

    def mix(j, slot):
        mixed[...] = mixed[...] * fades[slot][...] + jnp.dot(
            weights[slot][...], v_all[pl.ds(starting(j), block), :HD], preferred_element_type=jnp.float32
        )

    def weigh(i, j, fresh, slot, diagonal, bounded):
        lane = lax.broadcasted_iota(jnp.int32, (part, HD), 1)
        down = lax.broadcasted_iota(jnp.int32, (part, HD), 0)
        for r in range(0, block, part):
            here = slice(r, r + part)
            if bounded:
                begin = begins[pl.ds(pl.multiple_of(i * block + r, part), part), :] - starting(j) - lane
            columns = []
            for n, cols in enumerate(lanes):
                if diagonal and n * HD >= r + part:
                    break
                raw = scores[slot][here, cols]
                if bounded:
                    raw = jnp.where(begin <= n * HD, raw, NEG)
                if diagonal and (n + 1) * HD > r + 1:
                    raw = jnp.where(lane - down <= r - n * HD, raw, NEG)
                columns.append(raw)
            peak = functools.reduce(jnp.maximum, columns)
            old = jnp.where(fresh, NEG, top[here, :])
            new = jnp.maximum(old, jnp.max(peak, axis=1, keepdims=True))
            fade = jnp.exp2(old - new)
            total = totals[1 - slot][here, :] * fade
            for n, cols in enumerate(lanes):
                if n < len(columns):
                    weight = jnp.exp2(columns[n] - new)
                    total += weight
                    weights[slot][here, cols] = weight.astype(jnp.bfloat16)
                else:
                    weights[slot][here, cols] = jnp.zeros((part, HD), jnp.bfloat16)
            top[here, :] = new
            fades[slot][here, :] = fade
            totals[slot][here, :] = total

    def finish(i, slot):
        total = jnp.sum(totals[slot][...], axis=1, keepdims=True)
        v_all[pl.ds(starting(i), block), HD:] = (mixed[...] / total).astype(jnp.bfloat16)

    def step(state, slot):
        last_i, last_j, i, j = state
        done = j == i
        next_i = jnp.where(done, jnp.minimum(i + 1, blocks - 1), i)
        next_j = jnp.where(done, low_of(next_i), j + 1)
        bounded = high_of(i) > j * block
        fresh = j == low_of(i)

        def work(diagonal, bounded):
            mix(last_j, 1 - slot)
            score(next_i, next_j, 1 - slot)
            weigh(i, j, fresh, slot, diagonal, bounded)

        @pl.when(done & bounded)
        def _():
            work(True, True)

        @pl.when(done & jnp.logical_not(bounded))
        def _():
            work(True, False)

        @pl.when(jnp.logical_not(done) & bounded)
        def _():
            work(False, True)

        @pl.when(jnp.logical_not(done | bounded))
        def _():
            work(False, False)

        @pl.when(last_j == last_i)
        def _():
            finish(last_i, 1 - slot)

        return i, j, next_i, next_j

    pairs = blocks * (blocks + 1) // 2
    for i in range(blocks):
        pairs -= low_of(i)
    mixed[...] = jnp.zeros_like(mixed)
    for slot in range(2):
        weights[slot][...] = jnp.zeros_like(weights[slot])
        fades[slot][...] = jnp.zeros_like(fades[slot])
        totals[slot][...] = jnp.zeros_like(totals[slot])
    top[...] = jnp.full_like(top, NEG)
    score(0, 0, 0)

    def two_steps(n, state):
        middle = step(state, 0)
        after = step_if(2 * n + 1 < pairs, middle)
        return after

    def step_if(more, state):
        _, _, i, j = state
        done = j == i
        next_i = jnp.where(done, jnp.minimum(i + 1, blocks - 1), i)
        next_j = jnp.where(done, low_of(next_i), j + 1)

        @pl.when(more)
        def _():
            step(state, 1)

        return i, j, next_i, next_j

    zero = jnp.int32(0)
    lax.fori_loop(0, (pairs + 1) // 2, two_steps, (zero + 1, zero, zero, zero))

    for slot in range(2):

        @pl.when(pairs % 2 == 1 - slot)
        def _():
            mix(blocks - 1, slot)
            finish(blocks - 1, slot)

    for k in range(span):
        owner = lax.rem(number_ref[0] + k, span)
        out_refs[k][...] = v_all[pl.ds(pl.multiple_of(owner * rows, SUB), rows), HD:]


def attend(received, after, numbers, places, first, rows, span, win, block):
    devices, total, _ = received.shape
    length = span * rows
    vmem = pl.BlockSpec(memory_space=pltpu.VMEM)
    smem = pl.BlockSpec(memory_space=pltpu.SMEM)
    narrow = pltpu.VMEM((block, HD), jnp.float32)
    return pl.pallas_call(
        functools.partial(attend_kernel, rows, span, win, block),
        out_shape=[jax.ShapeDtypeStruct((rows, HD), jnp.bfloat16)] * span,
        in_specs=[smem] + [vmem] * 3 + [pl.BlockSpec(memory_space=pl.ANY)] * len(after),
        out_specs=[vmem] * span,
        scratch_shapes=[
            pltpu.VMEM((length, 2 * HD), jnp.bfloat16),
            pltpu.VMEM((length, 2 * HD), jnp.bfloat16),
            pltpu.VMEM((length, 2 * HD), jnp.bfloat16),
            [pltpu.VMEM((devices * win, 3 * HD), jnp.bfloat16)] * 2,
            pltpu.VMEM((length, HD), jnp.int32),
            narrow,
            narrow,
            [pltpu.VMEM((block, block), jnp.float32)] * 2,
            [pltpu.VMEM((block, block), jnp.bfloat16)] * 2,
            [narrow] * 2,
            [narrow] * 2,
        ],
        compiler_params=pltpu.CompilerParams(vmem_limit_bytes=VMEM_LIMIT),
        cost_estimate=pl.CostEstimate(
            flops=2 * length * devices * win * 3 * HD + 8 * length * length * HD,
            bytes_accessed=2 * (devices * total * 3 * HD + length * HD),
            transcendentals=length * length // 2,
        ),
        name="attend_head",
    )(numbers, places, first.reshape(length // HD, HD), received, *after)


def join_kernel(span, own_ref, *refs):
    out_ref = refs[-1]
    for n, ref in enumerate(refs[:-1]):
        head = n // span * span + lax.rem(own_ref[0] + span - n % span, span)
        out_ref[:, pl.ds(pl.multiple_of(head * HD, HD), HD)] = ref[...]


def join_heads(own, pieces, span):
    vmem = pl.BlockSpec(memory_space=pltpu.VMEM)
    smem = pl.BlockSpec(memory_space=pltpu.SMEM)
    rows = pieces[0].shape[0]
    return pl.pallas_call(
        functools.partial(join_kernel, span),
        out_shape=jax.ShapeDtypeStruct((rows, len(pieces) * HD), jnp.bfloat16),
        in_specs=[smem] + [vmem] * len(pieces),
        out_specs=vmem,
        compiler_params=pltpu.CompilerParams(vmem_limit_bytes=VMEM_LIMIT),
        name="join_heads",
    )(own, *pieces)


def body(queries, keys, values, target_row, doc_lengths):
    rows, width = queries.shape
    group = width // HD
    devices = lax.axis_size("seq")
    span = max(group // 2, 1)
    units = devices // span
    each = group // span
    length = span * rows
    pair_most = 3 * rows // (2 * devices)
    mean = rows // units
    most = min(pair_most * span, rows)
    usual = min(mean + mean // 16, most)
    index = lax.axis_index("seq")
    own = (index % span).astype(jnp.int32).reshape(1)
    unit_start = index // span * length

    docs = jnp.arange(doc_lengths.shape[0])
    starts = jnp.sum(jnp.where(docs[:, None] < docs[None, :], doc_lengths[:, None], 0), axis=0)
    positions = unit_start + jnp.arange(length, dtype=jnp.int32)
    first = jnp.max(jnp.where(starts[None, :] <= positions[:, None], starts[None, :], 0), axis=1)
    first = jnp.maximum(first - unit_start, 0)
    block = math.gcd(length, 512)
    settings = jnp.concatenate([own, first[::block] // block, first[block - 1 :: block]])

    def homeward(piece, shift):
        if shift == 0:
            return piece
        route = [
            (u * span + m, u * span + (m + shift) % span) for u in range(units) for m in range(span)
        ]
        return lax.ppermute(piece, "seq", route)

    def attended(cap):
        total = rounded_up(cap + 3, SUB)
        win = SUB
        while win < pair_most + SUB - 1:
            win *= 2
        win = min(total, win)
        pieces = []
        after = []
        for chunk in range(each):
            sent = sort_rows(queries, keys, values, target_row, units, span, cap, total, chunk)
            received = lax.all_to_all(sent, "seq", split_axis=0, concat_axis=0, tiled=True)
            if chunk == 0:
                offsets, places, crowded = plan_rows(received, devices, span, rows, total, win)
                numbers = jnp.concatenate([settings, offsets])
            heads = attend(received, after, numbers, places, first, rows, span, win, block)
            after = [homeward(heads[shift], shift) for shift in range(span)]
            pieces += after
        return pieces, crowded

    pieces, crowded = attended(usual)
    if usual == most:
        return join_heads(own, pieces, span)
    return lax.cond(
        crowded,
        lambda: join_heads(own, attended(most)[0], span),
        lambda: join_heads(own, pieces, span),
    )


def solution(mesh):
    in_specs = (P("seq", "head"), P("seq", "head"), P("seq", "head"), P("seq"), P())
    out_specs = P("seq", "head")
    return jax.shard_map(body, mesh=mesh, in_specs=in_specs, out_specs=out_specs, check_vma=False)
```

profile of v0, /device:TPU:0, one launch (start us, length us, event | category | flops | bytes accessed | tf_op | source)
XLA Modules:
  0.0 164.6 jit_solution(5128018617299892035)
XLA Ops:
  0.0 4.8 %sort_rows.6 = bf16[2,8,208,384]{3,2,1,0:T(8,128)(2,1)} custom-call(s32[3,128]{1,0:T(4,128)} %bitcast.15, bf16[384,2048]{1,0:T(8,128)(2,1)} %q_ref.3, bf16[384,2048]{1,0:T(8,128)(2,1)} %k_ref.3, bf16[384,2048]{1,0:T(8,128)(2,1)} %v_ref.3), custom_call_target="tpu_custom_call" | custom-call | flops 981467136 | bytes 4915200 | tf_op jit(solution)/shard_map/sort_rows/pallas_call | solution.py:76
  4.8 7.5 %all-to-all-start.2 = ((bf16[16,208,384]{2,1,0:T(8,128)(2,1)}), bf16[16,208,384]{2,1,0:T(8,128)(2,1)S(1)}, u32[]{:S(2)}, u32[]{:S(2)}) async-start(bf16[16,208,384]{2,1,0:T(8,128)(2,1)} %bitcast.14), calls=%async_computation.2 | async-start | bytes 5111808 | tf_op jit(solution)/shard_map/all_to_all | solution.py:432
  12.4 4.8 %sort_rows.7 = bf16[2,8,208,384]{3,2,1,0:T(8,128)(2,1)} custom-call(s32[3,128]{1,0:T(4,128)S(1)} %bitcast.16, bf16[384,2048]{1,0:T(8,128)(2,1)} %q_ref.3, bf16[384,2048]{1,0:T(8,128)(2,1)} %k_ref.3, bf16[384,2048]{1,0:T(8,128)(2,1)} %v_ref.3), custom_call_target="tpu_custom_call" | custom-call | flops 981467136 | bytes 4915200 | tf_op jit(solution)/shard_map/sort_rows/pallas_call | solution.py:76
  17.2 44.3 %all-to-all-done.2.refs_0_.recv_ref = bf16[16,208,384]{2,1,0:T(8,128)(2,1)S(1)} async-done(((bf16[16,208,384]{2,1,0:T(8,128)(2,1)}), bf16[16,208,384]{2,1,0:T(8,128)(2,1)S(1)}, u32[]{:S(2)}, u32[]{:S(2)}) %all-to-all-start.2) | async-done | bytes 2555936 | tf_op jit(solution)/shard_map/all_to_all | solution.py:432
  61.4 13.2 %all-to-all-start.3 = ((bf16[16,208,384]{2,1,0:T(8,128)(2,1)}), bf16[16,208,384]{2,1,0:T(8,128)(2,1)}, u32[]{:S(2)}, u32[]{:S(2)}) async-start(bf16[16,208,384]{2,1,0:T(8,128)(2,1)} %bitcast.13), calls=%async_computation.3 | async-start | bytes 5111808 | tf_op jit(solution)/shard_map/all_to_all | solution.py:432
  74.7 0.1 select_reduce_fusion.1
  74.8 0.2 select_reduce_fusion
  75.0 0.1 slice.12
  75.1 0.1 slice.13
  75.2 0.8 plan_rows.3
  76.0 0.2 slice_reduce_fusion.1
  76.2 0.1 reshape_squeeze.3
  76.3 0.1 pad_add_fusion.1.number_ref
  76.4 16.3 %attend_head.6 = (bf16[384,128]{1,0:T(8,128)(2,1)S(1)}, bf16[384,128]{1,0:T(8,128)(2,1)S(1)}, bf16[384,128]{1,0:T(8,128)(2,1)S(1)}, bf16[384,128]{1,0:T(8,128)(2...) custom-call(s32[141]{0:T(256)S(1)} %pad_add_fusion.1.number_ref, ...), custom_call_target="tpu_custom_call" | custom-call | flops 12079595520 | bytes 3342336 | tf_op jit(solution)/shard_map/attend_head/pallas_call | solution.py:341
  92.6 0.4 collective-permute-start.14
  93.0 1.7 %collective-permute-start.15 = (bf16[384,128]{1,0:T(8,128)(2,1)S(1)}, bf16[384,128]{1,0:T(8,128)(2,1)S(1)}, u32[]{:S(2)}, u32[]{:S(2)}) collective-permute-start(bf16[384,128]{1,0:T(8,128)(2,1)S(1)} %get-tuple-element.122), channel_id=1, source_target_pairs={{0,4},{2,6},{4,8},{6,10},{8,12},{10,14},{12,0},{14,2},{16,20},{18,... | collective-permute-start | bytes 294920 | tf_op jit(solution)/shard_map/ppermute | solution.py:420
  94.7 2.2 %collective-permute-start.16 = (bf16[384,128]{1,0:T(8,128)(2,1)S(1)}, bf16[384,128]{1,0:T(8,128)(2,1)S(1)}, u32[]{:S(2)}, u32[]{:S(2)}) collective-permute-start(bf16[384,128]{1,0:T(8,128)(2,1)S(1)} %get-tuple-element.123), channel_id=1, source_target_pairs={{0,6},{2,8},{4,10},{6,12},{8,14},{10,0},{12,2},{14,4},{16,22},{18,... | collective-permute-start | bytes 294920 | tf_op jit(solution)/shard_map/ppermute | solution.py:420
  96.9 0.6 collective-permute-start.17
  97.5 0.1 collective-permute-start.18
  97.6 13.6 %collective-permute-done.14.refs_1_ = bf16[384,128]{1,0:T(8,128)(2,1)S(1)} collective-permute-done((bf16[384,128]{1,0:T(8,128)(2,1)S(1)}, bf16[384,128]{1,0:T(8,128)(2,1)S(1)}, u32[]{:S(2)}, u32[]{:S(2)}) %collective-permute-start.14) | collective-permute-done | bytes 98336 | tf_op jit(solution)/shard_map/ppermute | solution.py:420
  111.2 0.0 collective-permute-start.19
  111.2 0.9 collective-permute-done.15.refs_2_
  112.1 0.4 collective-permute-start.20
  112.6 11.5 %all-to-all-done.3.recv_ref = bf16[16,208,384]{2,1,0:T(8,128)(2,1)} async-done(((bf16[16,208,384]{2,1,0:T(8,128)(2,1)}), bf16[16,208,384]{2,1,0:T(8,128)(2,1)}, u32[]{:S(2)}, u32[]{:S(2)}) %all-to-all-start.3) | async-done | bytes 2555936 | tf_op jit(solution)/shard_map/all_to_all | solution.py:432
  124.1 0.0 collective-permute-done.16.refs_3_
  124.1 0.0 collective-permute-done.17.refs_4_
  124.1 0.0 collective-permute-done.18.refs_5_
  124.1 0.0 collective-permute-done.19.refs_6_
  124.1 1.3 collective-permute-done.20.refs_7_
  125.4 0.6 copy-done.2
  126.0 17.6 %attend_head.7 = (bf16[384,128]{1,0:T(8,128)(2,1)S(1)}, bf16[384,128]{1,0:T(8,128)(2,1)S(1)}, bf16[384,128]{1,0:T(8,128)(2,1)S(1)}, bf16[384,128]{1,0:T(8,128)(2...) custom-call(s32[141]{0:T(256)S(1)} %pad_add_fusion.1.number_ref, ...), custom_call_target="tpu_custom_call" | custom-call | flops 12079595520 | bytes 3342336 | tf_op jit(solution)/shard_map/attend_head/pallas_call | solution.py:341
  143.6 1.0 collective-permute-start.21
  144.5 4.9 %collective-permute-start.22 = (bf16[384,128]{1,0:T(8,128)(2,1)S(1)}, bf16[384,128]{1,0:T(8,128)(2,1)S(1)}, u32[]{:S(2)}, u32[]{:S(2)}) collective-permute-start(bf16[384,128]{1,0:T(8,128)(2,1)S(1)} %get-tuple-element.130), channel_id=1, source_target_pairs={{0,4},{2,6},{4,8},{6,10},{8,12},{10,14},{12,0},{14,2},{16,20},{18,... | collective-permute-start | bytes 294920 | tf_op jit(solution)/shard_map/ppermute | solution.py:420
  149.5 5.2 %collective-permute-start.23 = (bf16[384,128]{1,0:T(8,128)(2,1)S(1)}, bf16[384,128]{1,0:T(8,128)(2,1)S(1)}, u32[]{:S(2)}, u32[]{:S(2)}) collective-permute-start(bf16[384,128]{1,0:T(8,128)(2,1)S(1)} %get-tuple-element.131), channel_id=1, source_target_pairs={{0,6},{2,8},{4,10},{6,12},{8,14},{10,0},{12,2},{14,4},{16,22},{18,... | collective-permute-start | bytes 294920 | tf_op jit(solution)/shard_map/ppermute | solution.py:420
  154.6 0.0 collective-permute-start.24
  154.6 0.8 collective-permute-start.25
  155.5 0.3 collective-permute-done.21
  155.8 1.7 %collective-permute-start.26 = (bf16[384,128]{1,0:T(8,128)(2,1)S(1)}, bf16[384,128]{1,0:T(8,128)(2,1)S(1)}, u32[]{:S(2)}, u32[]{:S(2)}) collective-permute-start(bf16[384,128]{1,0:T(8,128)(2,1)S(1)} %get-tuple-element.134), channel_id=1, source_target_pairs={{0,12},{2,14},{4,0},{6,2},{8,4},{10,6},{12,8},{14,10},{16,28},{18,... | collective-permute-start | bytes 294920 | tf_op jit(solution)/shard_map/ppermute | solution.py:420
  157.4 0.0 collective-permute-done.22
  157.4 1.8 %collective-permute-start.27 = (bf16[384,128]{1,0:T(8,128)(2,1)S(1)}, bf16[384,128]{1,0:T(8,128)(2,1)S(1)}, u32[]{:S(2)}, u32[]{:S(2)}) collective-permute-start(bf16[384,128]{1,0:T(8,128)(2,1)S(1)} %get-tuple-element.135), channel_id=1, source_target_pairs={{0,14},{2,0},{4,2},{6,4},{8,6},{10,8},{12,10},{14,12},{16,30},{18,... | collective-permute-start | bytes 294920 | tf_op jit(solution)/shard_map/ppermute | solution.py:420
  159.2 0.6 pad_add_fusion.2
  160.4 0.0 collective-permute-done.23
  160.4 0.0 collective-permute-done.24
  160.4 0.0 collective-permute-done.25
  160.5 1.4 collective-permute-done.26
  161.9 1.1 collective-permute-done.27
  163.0 1.6 conditional.1
  163.0 1.6 join_heads.2
  (13 shorter events, 0.0 us)
Async XLA Ops:
  4.8 7.5 %copy-start.4 = (s32[384]{0:T(512)S(1)}, s32[384]{0:T(512)}, u32[]{:S(2)}) copy-start(s32[384]{0:T(512)} %param.10) | copy-start | bytes 4612
  4.8 56.6 %all-to-all-start.2 = ((bf16[16,208,384]{2,1,0:T(8,128)(2,1)}), bf16[16,208,384]{2,1,0:T(8,128)(2,1)S(1)}, u32[]{:S(2)}, u32[]{:S(2)}) async-start(bf16[16,208,384]{2,1,0:T(8,128)(2,1)} %bitcast.14), calls=%async_computation.2 | async-start | bytes 5111808 | tf_op jit(solution)/shard_map/all_to_all | solution.py:432
  61.4 13.3 %copy-start.6 = (s32[32]{0:T(128)S(1)}, s32[32]{0:T(128)}, u32[]{:S(2)}) copy-start(s32[32]{0:T(128)} %param.11) | copy-start | bytes 388
  61.4 62.6 %all-to-all-start.3 = ((bf16[16,208,384]{2,1,0:T(8,128)(2,1)}), bf16[16,208,384]{2,1,0:T(8,128)(2,1)}, u32[]{:S(2)}, u32[]{:S(2)}) async-start(bf16[16,208,384]{2,1,0:T(8,128)(2,1)} %bitcast.13), calls=%async_computation.3 | async-start | bytes 5111808 | tf_op jit(solution)/shard_map/all_to_all | solution.py:432
  92.6 18.6 %collective-permute-start.14 = (bf16[384,128]{1,0:T(8,128)(2,1)S(1)}, bf16[384,128]{1,0:T(8,128)(2,1)S(1)}, u32[]{:S(2)}, u32[]{:S(2)}) collective-permute-start(bf16[384,128]{1,0:T(8,128)(2,1)S(1)} %get-tuple-element.121), channel_id=1, source_target_pairs={{0,2},{2,4},{4,6},{6,8},{8,10},{10,12},{12,14},{14,0},{16,18},{18,... | collective-permute-start | bytes 294920 | tf_op jit(solution)/shard_map/ppermute | solution.py:420
  93.0 19.1 %collective-permute-start.15 = (bf16[384,128]{1,0:T(8,128)(2,1)S(1)}, bf16[384,128]{1,0:T(8,128)(2,1)S(1)}, u32[]{:S(2)}, u32[]{:S(2)}) collective-permute-start(bf16[384,128]{1,0:T(8,128)(2,1)S(1)} %get-tuple-element.122), channel_id=1, source_target_pairs={{0,4},{2,6},{4,8},{6,10},{8,12},{10,14},{12,0},{14,2},{16,20},{18,... | collective-permute-start | bytes 294920 | tf_op jit(solution)/shard_map/ppermute | solution.py:420
  94.7 29.4 %collective-permute-start.16 = (bf16[384,128]{1,0:T(8,128)(2,1)S(1)}, bf16[384,128]{1,0:T(8,128)(2,1)S(1)}, u32[]{:S(2)}, u32[]{:S(2)}) collective-permute-start(bf16[384,128]{1,0:T(8,128)(2,1)S(1)} %get-tuple-element.123), channel_id=1, source_target_pairs={{0,6},{2,8},{4,10},{6,12},{8,14},{10,0},{12,2},{14,4},{16,22},{18,... | collective-permute-start | bytes 294920 | tf_op jit(solution)/shard_map/ppermute | solution.py:420
  96.9 27.2 %collective-permute-start.17 = (bf16[384,128]{1,0:T(8,128)(2,1)S(1)}, bf16[384,128]{1,0:T(8,128)(2,1)S(1)}, u32[]{:S(2)}, u32[]{:S(2)}) collective-permute-start(bf16[384,128]{1,0:T(8,128)(2,1)S(1)} %get-tuple-element.124), channel_id=1, source_target_pairs={{0,8},{2,10},{4,12},{6,14},{8,0},{10,2},{12,4},{14,6},{16,24},{18,... | collective-permute-start | bytes 294920 | tf_op jit(solution)/shard_map/ppermute | solution.py:420
  97.5 26.6 %collective-permute-start.18 = (bf16[384,128]{1,0:T(8,128)(2,1)S(1)}, bf16[384,128]{1,0:T(8,128)(2,1)S(1)}, u32[]{:S(2)}, u32[]{:S(2)}) collective-permute-start(bf16[384,128]{1,0:T(8,128)(2,1)S(1)} %get-tuple-element.125), channel_id=1, source_target_pairs={{0,10},{2,12},{4,14},{6,0},{8,2},{10,4},{12,6},{14,8},{16,26},{18,... | collective-permute-start | bytes 294920 | tf_op jit(solution)/shard_map/ppermute | solution.py:420
  111.2 12.9 %collective-permute-start.19 = (bf16[384,128]{1,0:T(8,128)(2,1)S(1)}, bf16[384,128]{1,0:T(8,128)(2,1)S(1)}, u32[]{:S(2)}, u32[]{:S(2)}) collective-permute-start(bf16[384,128]{1,0:T(8,128)(2,1)S(1)} %get-tuple-element.126), channel_id=1, source_target_pairs={{0,12},{2,14},{4,0},{6,2},{8,4},{10,6},{12,8},{14,10},{16,28},{18,... | collective-permute-start | bytes 294920 | tf_op jit(solution)/shard_map/ppermute | solution.py:420
  112.1 13.2 %collective-permute-start.20 = (bf16[384,128]{1,0:T(8,128)(2,1)S(1)}, bf16[384,128]{1,0:T(8,128)(2,1)S(1)}, u32[]{:S(2)}, u32[]{:S(2)}) collective-permute-start(bf16[384,128]{1,0:T(8,128)(2,1)S(1)} %get-tuple-element.127), channel_id=1, source_target_pairs={{0,14},{2,0},{4,2},{6,4},{8,6},{10,8},{12,10},{14,12},{16,30},{18,... | collective-permute-start | bytes 294920 | tf_op jit(solution)/shard_map/ppermute | solution.py:420
  125.4 0.6 copy-start.2
  126.0 36.9 %copy-start = (bf16[384,2048]{1,0:T(8,128)(2,1)S(1)}, bf16[384,2048]{1,0:T(8,128)(2,1)}, u32[]{:S(2)}) copy-start(bf16[384,2048]{1,0:T(8,128)(2,1)} %q_ref.3) | copy-start | bytes 4718596
  126.0 36.9 %copy-start.3 = (bf16[384,128]{1,0:T(8,128)(2,1)S(1)}, bf16[384,128]{1,0:T(8,128)(2,1)}, u32[]{:S(2)}) copy-start(bf16[384,128]{1,0:T(8,128)(2,1)} %copy-done.2) | copy-start | bytes 294916
  143.6 12.2 %collective-permute-start.21 = (bf16[384,128]{1,0:T(8,128)(2,1)S(1)}, bf16[384,128]{1,0:T(8,128)(2,1)S(1)}, u32[]{:S(2)}, u32[]{:S(2)}) collective-permute-start(bf16[384,128]{1,0:T(8,128)(2,1)S(1)} %get-tuple-element.129), channel_id=1, source_target_pairs={{0,2},{2,4},{4,6},{6,8},{8,10},{10,12},{12,14},{14,0},{16,18},{18,... | collective-permute-start | bytes 294920 | tf_op jit(solution)/shard_map/ppermute | solution.py:420
  144.5 12.9 %collective-permute-start.22 = (bf16[384,128]{1,0:T(8,128)(2,1)S(1)}, bf16[384,128]{1,0:T(8,128)(2,1)S(1)}, u32[]{:S(2)}, u32[]{:S(2)}) collective-permute-start(bf16[384,128]{1,0:T(8,128)(2,1)S(1)} %get-tuple-element.130), channel_id=1, source_target_pairs={{0,4},{2,6},{4,8},{6,10},{8,12},{10,14},{12,0},{14,2},{16,20},{18,... | collective-permute-start | bytes 294920 | tf_op jit(solution)/shard_map/ppermute | solution.py:420
  149.5 10.9 %collective-permute-start.23 = (bf16[384,128]{1,0:T(8,128)(2,1)S(1)}, bf16[384,128]{1,0:T(8,128)(2,1)S(1)}, u32[]{:S(2)}, u32[]{:S(2)}) collective-permute-start(bf16[384,128]{1,0:T(8,128)(2,1)S(1)} %get-tuple-element.131), channel_id=1, source_target_pairs={{0,6},{2,8},{4,10},{6,12},{8,14},{10,0},{12,2},{14,4},{16,22},{18,... | collective-permute-start | bytes 294920 | tf_op jit(solution)/shard_map/ppermute | solution.py:420
  154.6 5.8 %collective-permute-start.24 = (bf16[384,128]{1,0:T(8,128)(2,1)S(1)}, bf16[384,128]{1,0:T(8,128)(2,1)S(1)}, u32[]{:S(2)}, u32[]{:S(2)}) collective-permute-start(bf16[384,128]{1,0:T(8,128)(2,1)S(1)} %get-tuple-element.132), channel_id=1, source_target_pairs={{0,8},{2,10},{4,12},{6,14},{8,0},{10,2},{12,4},{14,6},{16,24},{18,... | collective-permute-start | bytes 294920 | tf_op jit(solution)/shard_map/ppermute | solution.py:420
  154.6 5.8 %collective-permute-start.25 = (bf16[384,128]{1,0:T(8,128)(2,1)S(1)}, bf16[384,128]{1,0:T(8,128)(2,1)S(1)}, u32[]{:S(2)}, u32[]{:S(2)}) collective-permute-start(bf16[384,128]{1,0:T(8,128)(2,1)S(1)} %get-tuple-element.133), channel_id=1, source_target_pairs={{0,10},{2,12},{4,14},{6,0},{8,2},{10,4},{12,6},{14,8},{16,26},{18,... | collective-permute-start | bytes 294920 | tf_op jit(solution)/shard_map/ppermute | solution.py:420
  155.8 6.1 %collective-permute-start.26 = (bf16[384,128]{1,0:T(8,128)(2,1)S(1)}, bf16[384,128]{1,0:T(8,128)(2,1)S(1)}, u32[]{:S(2)}, u32[]{:S(2)}) collective-permute-start(bf16[384,128]{1,0:T(8,128)(2,1)S(1)} %get-tuple-element.134), channel_id=1, source_target_pairs={{0,12},{2,14},{4,0},{6,2},{8,4},{10,6},{12,8},{14,10},{16,28},{18,... | collective-permute-start | bytes 294920 | tf_op jit(solution)/shard_map/ppermute | solution.py:420
  157.4 5.5 %collective-permute-start.27 = (bf16[384,128]{1,0:T(8,128)(2,1)S(1)}, bf16[384,128]{1,0:T(8,128)(2,1)S(1)}, u32[]{:S(2)}, u32[]{:S(2)}) collective-permute-start(bf16[384,128]{1,0:T(8,128)(2,1)S(1)} %get-tuple-element.135), channel_id=1, source_target_pairs={{0,14},{2,0},{4,2},{6,4},{8,6},{10,8},{12,10},{14,12},{16,30},{18,... | collective-permute-start | bytes 294920 | tf_op jit(solution)/shard_map/ppermute | solution.py:420
where the time goes:
time: 165 us
  waiting for transfers between devices  74.4 us (45%)
  Pallas kernels  45.9 us (28%)
  starting transfers between devices  41.5 us (25%)
    all_to_all x2, waiting for transfers between devices, attended(): lax.all_to_all(sent, 'seq', split_axis=0, concat_axis=0, tiled=True)  55.8 us
    pallas_call x2, Pallas kernels, attend(): pl.pallas_call(functools.partial(attend_kernel, rows, span, win, block),...  33.8 us
    ppermute x14, starting transfers between devices, homeward(): return lax.ppermute(piece, 'seq', route)  20.8 us
    all_to_all x2, starting transfers between devices, attended(): lax.all_to_all(sent, 'seq', split_axis=0, concat_axis=0, tiled=True)  20.7 us
    ppermute x14, waiting for transfers between devices, homeward(): return lax.ppermute(piece, 'seq', route)  18.6 us
    pallas_call x2, Pallas kernels, sort_rows(): pl.pallas_call(functools.partial(sort_kernel, units, span * rows, cap, to...  9.65 us
  transfers between devices with their start and end apart: 16, of which 8 were waited for; matrix products, arithmetic and copies ran while one was open for 1% of the time, Pallas kernels for 13%

commit v1 on v0

--- a/solution.py
+++ b/solution.py
@@ -13,7 +13,7 @@
 BASE = 64
 NEG = -1e30
 EXP2_SCALE = math.log2(math.e) / math.sqrt(HD)
-VMEM_LIMIT = 40 * 1024 * 1024
+VMEM_LIMIT = 24 * 1024 * 1024
 SORT_LIMIT = 60 * 1024 * 1024
 
 
@@ -168,7 +168,7 @@
     def high_of(i):
         return number_ref[1 + blocks + i]
 
-    part = min(32, block)
+    part = min(64, block)
 
     @pl.when(high_of(blocks - 1) > 0)
     def _():

time: 165 us -> 165 us (level)
  no operation moved by 1% of the time
where the time goes in v1:
time: 165 us
  waiting for transfers between devices  74.4 us (45%)
  Pallas kernels  45.9 us (28%)
  starting transfers between devices  41.5 us (25%)
    all_to_all x2, waiting for transfers between devices, attended(): lax.all_to_all(sent, 'seq', split_axis=0, concat_axis=0, tiled=True)  55.8 us
    pallas_call x2, Pallas kernels, attend(): pl.pallas_call(functools.partial(attend_kernel, rows, span, win, block),...  33.8 us
    ppermute x14, starting transfers between devices, homeward(): return lax.ppermute(piece, 'seq', route)  20.8 us
    all_to_all x2, starting transfers between devices, attended(): lax.all_to_all(sent, 'seq', split_axis=0, concat_axis=0, tiled=True)  20.7 us
    ppermute x14, waiting for transfers between devices, homeward(): return lax.ppermute(piece, 'seq', route)  18.6 us
    pallas_call x2, Pallas kernels, sort_rows(): pl.pallas_call(functools.partial(sort_kernel, units, span * rows, cap, to...  9.65 us
  transfers between devices with their start and end apart: 16, of which 8 were waited for; matrix products, arithmetic and copies ran while one was open for 1% of the time, Pallas kernels for 13%

profile of v1, /device:TPU:0, one launch (start us, length us, event | category | flops | bytes accessed | tf_op | source)
XLA Modules:
  0.0 164.6 jit_solution(5903209410076167861)
XLA Ops:
  0.0 4.8 %sort_rows.6 = bf16[2,8,208,384]{3,2,1,0:T(8,128)(2,1)} custom-call(s32[3,128]{1,0:T(4,128)} %bitcast.15, bf16[384,2048]{1,0:T(8,128)(2,1)} %q_ref.3, bf16[384,2048]{1,0:T(8,128)(2,1)} %k_ref.3, bf16[384,2048]{1,0:T(8,128)(2,1)} %v_ref.3), custom_call_target="tpu_custom_call" | custom-call | flops 981467136 | bytes 4915200 | tf_op jit(solution)/shard_map/sort_rows/pallas_call | solution.py:76
  4.8 7.5 %all-to-all-start.2 = ((bf16[16,208,384]{2,1,0:T(8,128)(2,1)}), bf16[16,208,384]{2,1,0:T(8,128)(2,1)S(1)}, u32[]{:S(2)}, u32[]{:S(2)}) async-start(bf16[16,208,384]{2,1,0:T(8,128)(2,1)} %bitcast.14), calls=%async_computation.2 | async-start | bytes 5111808 | tf_op jit(solution)/shard_map/all_to_all | solution.py:432
  12.4 4.8 %sort_rows.7 = bf16[2,8,208,384]{3,2,1,0:T(8,128)(2,1)} custom-call(s32[3,128]{1,0:T(4,128)S(1)} %bitcast.16, bf16[384,2048]{1,0:T(8,128)(2,1)} %q_ref.3, bf16[384,2048]{1,0:T(8,128)(2,1)} %k_ref.3, bf16[384,2048]{1,0:T(8,128)(2,1)} %v_ref.3), custom_call_target="tpu_custom_call" | custom-call | flops 981467136 | bytes 4915200 | tf_op jit(solution)/shard_map/sort_rows/pallas_call | solution.py:76
  17.2 44.3 %all-to-all-done.2.refs_0_.recv_ref = bf16[16,208,384]{2,1,0:T(8,128)(2,1)S(1)} async-done(((bf16[16,208,384]{2,1,0:T(8,128)(2,1)}), bf16[16,208,384]{2,1,0:T(8,128)(2,1)S(1)}, u32[]{:S(2)}, u32[]{:S(2)}) %all-to-all-start.2) | async-done | bytes 2555936 | tf_op jit(solution)/shard_map/all_to_all | solution.py:432
  61.4 13.2 %all-to-all-start.3 = ((bf16[16,208,384]{2,1,0:T(8,128)(2,1)}), bf16[16,208,384]{2,1,0:T(8,128)(2,1)}, u32[]{:S(2)}, u32[]{:S(2)}) async-start(bf16[16,208,384]{2,1,0:T(8,128)(2,1)} %bitcast.13), calls=%async_computation.3 | async-start | bytes 5111808 | tf_op jit(solution)/shard_map/all_to_all | solution.py:432
  74.7 0.1 select_reduce_fusion.1
  74.8 0.2 select_reduce_fusion
  75.0 0.1 slice.12
  75.1 0.1 slice.13
  75.2 0.8 plan_rows.3
  76.0 0.2 slice_reduce_fusion.1
  76.2 0.1 reshape_squeeze.3
  76.3 0.1 pad_add_fusion.1.number_ref
  76.4 16.3 %attend_head.6 = (bf16[384,128]{1,0:T(8,128)(2,1)S(1)}, bf16[384,128]{1,0:T(8,128)(2,1)S(1)}, bf16[384,128]{1,0:T(8,128)(2,1)S(1)}, bf16[384,128]{1,0:T(8,128)(2...) custom-call(s32[141]{0:T(256)S(1)} %pad_add_fusion.1.number_ref, ...), custom_call_target="tpu_custom_call" | custom-call | flops 12079595520 | bytes 3342336 | tf_op jit(solution)/shard_map/attend_head/pallas_call | solution.py:341
  92.6 0.4 collective-permute-start.14
  93.0 1.6 collective-permute-start.15
  94.7 2.2 %collective-permute-start.16 = (bf16[384,128]{1,0:T(8,128)(2,1)S(1)}, bf16[384,128]{1,0:T(8,128)(2,1)S(1)}, u32[]{:S(2)}, u32[]{:S(2)}) collective-permute-start(bf16[384,128]{1,0:T(8,128)(2,1)S(1)} %get-tuple-element.123), channel_id=1, source_target_pairs={{0,6},{2,8},{4,10},{6,12},{8,14},{10,0},{12,2},{14,4},{16,22},{18,... | collective-permute-start | bytes 294920 | tf_op jit(solution)/shard_map/ppermute | solution.py:420
  96.9 0.5 collective-permute-start.17
  97.5 0.2 collective-permute-start.18
  97.6 13.6 %collective-permute-done.14.refs_1_ = bf16[384,128]{1,0:T(8,128)(2,1)S(1)} collective-permute-done((bf16[384,128]{1,0:T(8,128)(2,1)S(1)}, bf16[384,128]{1,0:T(8,128)(2,1)S(1)}, u32[]{:S(2)}, u32[]{:S(2)}) %collective-permute-start.14) | collective-permute-done | bytes 98336 | tf_op jit(solution)/shard_map/ppermute | solution.py:420
  111.2 0.0 collective-permute-start.19
  111.2 0.9 collective-permute-done.15.refs_2_
  112.1 0.4 collective-permute-start.20
  112.6 11.5 %all-to-all-done.3.recv_ref = bf16[16,208,384]{2,1,0:T(8,128)(2,1)} async-done(((bf16[16,208,384]{2,1,0:T(8,128)(2,1)}), bf16[16,208,384]{2,1,0:T(8,128)(2,1)}, u32[]{:S(2)}, u32[]{:S(2)}) %all-to-all-start.3) | async-done | bytes 2555936 | tf_op jit(solution)/shard_map/all_to_all | solution.py:432
  124.1 0.0 collective-permute-done.16.refs_3_
  124.1 0.0 collective-permute-done.17.refs_4_
  124.1 0.0 collective-permute-done.18.refs_5_
  124.1 0.0 collective-permute-done.19.refs_6_
  124.1 1.3 collective-permute-done.20.refs_7_
  125.4 0.6 copy-done.2
  126.0 17.6 %attend_head.7 = (bf16[384,128]{1,0:T(8,128)(2,1)S(1)}, bf16[384,128]{1,0:T(8,128)(2,1)S(1)}, bf16[384,128]{1,0:T(8,128)(2,1)S(1)}, bf16[384,128]{1,0:T(8,128)(2...) custom-call(s32[141]{0:T(256)S(1)} %pad_add_fusion.1.number_ref, ...), custom_call_target="tpu_custom_call" | custom-call | flops 12079595520 | bytes 3342336 | tf_op jit(solution)/shard_map/attend_head/pallas_call | solution.py:341
  143.6 1.0 collective-permute-start.21
  144.6 4.9 %collective-permute-start.22 = (bf16[384,128]{1,0:T(8,128)(2,1)S(1)}, bf16[384,128]{1,0:T(8,128)(2,1)S(1)}, u32[]{:S(2)}, u32[]{:S(2)}) collective-permute-start(bf16[384,128]{1,0:T(8,128)(2,1)S(1)} %get-tuple-element.130), channel_id=1, source_target_pairs={{0,4},{2,6},{4,8},{6,10},{8,12},{10,14},{12,0},{14,2},{16,20},{18,... | collective-permute-start | bytes 294920 | tf_op jit(solution)/shard_map/ppermute | solution.py:420
  149.5 5.2 %collective-permute-start.23 = (bf16[384,128]{1,0:T(8,128)(2,1)S(1)}, bf16[384,128]{1,0:T(8,128)(2,1)S(1)}, u32[]{:S(2)}, u32[]{:S(2)}) collective-permute-start(bf16[384,128]{1,0:T(8,128)(2,1)S(1)} %get-tuple-element.131), channel_id=1, source_target_pairs={{0,6},{2,8},{4,10},{6,12},{8,14},{10,0},{12,2},{14,4},{16,22},{18,... | collective-permute-start | bytes 294920 | tf_op jit(solution)/shard_map/ppermute | solution.py:420
  154.6 0.0 collective-permute-start.24
  154.6 0.8 collective-permute-start.25
  155.5 0.3 collective-permute-done.21
  155.8 1.7 %collective-permute-start.26 = (bf16[384,128]{1,0:T(8,128)(2,1)S(1)}, bf16[384,128]{1,0:T(8,128)(2,1)S(1)}, u32[]{:S(2)}, u32[]{:S(2)}) collective-permute-start(bf16[384,128]{1,0:T(8,128)(2,1)S(1)} %get-tuple-element.134), channel_id=1, source_target_pairs={{0,12},{2,14},{4,0},{6,2},{8,4},{10,6},{12,8},{14,10},{16,28},{18,... | collective-permute-start | bytes 294920 | tf_op jit(solution)/shard_map/ppermute | solution.py:420
  157.4 0.0 collective-permute-done.22
  157.4 1.8 %collective-permute-start.27 = (bf16[384,128]{1,0:T(8,128)(2,1)S(1)}, bf16[384,128]{1,0:T(8,128)(2,1)S(1)}, u32[]{:S(2)}, u32[]{:S(2)}) collective-permute-start(bf16[384,128]{1,0:T(8,128)(2,1)S(1)} %get-tuple-element.135), channel_id=1, source_target_pairs={{0,14},{2,0},{4,2},{6,4},{8,6},{10,8},{12,10},{14,12},{16,30},{18,... | collective-permute-start | bytes 294920 | tf_op jit(solution)/shard_map/ppermute | solution.py:420
  159.3 0.6 pad_add_fusion.2
  160.4 0.0 collective-permute-done.23
  160.4 0.0 collective-permute-done.24
  160.5 0.0 collective-permute-done.25
  160.5 1.4 collective-permute-done.26
  161.9 1.1 collective-permute-done.27
  163.0 1.6 conditional.1
  163.0 1.6 join_heads.2
  (13 shorter events, 0.0 us)
Async XLA Ops:
  4.8 7.5 %copy-start.4 = (s32[384]{0:T(512)S(1)}, s32[384]{0:T(512)}, u32[]{:S(2)}) copy-start(s32[384]{0:T(512)} %param.10) | copy-start | bytes 4612
  4.8 56.6 %all-to-all-start.2 = ((bf16[16,208,384]{2,1,0:T(8,128)(2,1)}), bf16[16,208,384]{2,1,0:T(8,128)(2,1)S(1)}, u32[]{:S(2)}, u32[]{:S(2)}) async-start(bf16[16,208,384]{2,1,0:T(8,128)(2,1)} %bitcast.14), calls=%async_computation.2 | async-start | bytes 5111808 | tf_op jit(solution)/shard_map/all_to_all | solution.py:432
  61.4 13.3 %copy-start.6 = (s32[32]{0:T(128)S(1)}, s32[32]{0:T(128)}, u32[]{:S(2)}) copy-start(s32[32]{0:T(128)} %param.11) | copy-start | bytes 388
  61.4 62.6 %all-to-all-start.3 = ((bf16[16,208,384]{2,1,0:T(8,128)(2,1)}), bf16[16,208,384]{2,1,0:T(8,128)(2,1)}, u32[]{:S(2)}, u32[]{:S(2)}) async-start(bf16[16,208,384]{2,1,0:T(8,128)(2,1)} %bitcast.13), calls=%async_computation.3 | async-start | bytes 5111808 | tf_op jit(solution)/shard_map/all_to_all | solution.py:432
  92.6 18.6 %collective-permute-start.14 = (bf16[384,128]{1,0:T(8,128)(2,1)S(1)}, bf16[384,128]{1,0:T(8,128)(2,1)S(1)}, u32[]{:S(2)}, u32[]{:S(2)}) collective-permute-start(bf16[384,128]{1,0:T(8,128)(2,1)S(1)} %get-tuple-element.121), channel_id=1, source_target_pairs={{0,2},{2,4},{4,6},{6,8},{8,10},{10,12},{12,14},{14,0},{16,18},{18,... | collective-permute-start | bytes 294920 | tf_op jit(solution)/shard_map/ppermute | solution.py:420
  93.0 19.1 %collective-permute-start.15 = (bf16[384,128]{1,0:T(8,128)(2,1)S(1)}, bf16[384,128]{1,0:T(8,128)(2,1)S(1)}, u32[]{:S(2)}, u32[]{:S(2)}) collective-permute-start(bf16[384,128]{1,0:T(8,128)(2,1)S(1)} %get-tuple-element.122), channel_id=1, source_target_pairs={{0,4},{2,6},{4,8},{6,10},{8,12},{10,14},{12,0},{14,2},{16,20},{18,... | collective-permute-start | bytes 294920 | tf_op jit(solution)/shard_map/ppermute | solution.py:420
  94.7 29.4 %collective-permute-start.16 = (bf16[384,128]{1,0:T(8,128)(2,1)S(1)}, bf16[384,128]{1,0:T(8,128)(2,1)S(1)}, u32[]{:S(2)}, u32[]{:S(2)}) collective-permute-start(bf16[384,128]{1,0:T(8,128)(2,1)S(1)} %get-tuple-element.123), channel_id=1, source_target_pairs={{0,6},{2,8},{4,10},{6,12},{8,14},{10,0},{12,2},{14,4},{16,22},{18,... | collective-permute-start | bytes 294920 | tf_op jit(solution)/shard_map/ppermute | solution.py:420
  96.9 27.2 %collective-permute-start.17 = (bf16[384,128]{1,0:T(8,128)(2,1)S(1)}, bf16[384,128]{1,0:T(8,128)(2,1)S(1)}, u32[]{:S(2)}, u32[]{:S(2)}) collective-permute-start(bf16[384,128]{1,0:T(8,128)(2,1)S(1)} %get-tuple-element.124), channel_id=1, source_target_pairs={{0,8},{2,10},{4,12},{6,14},{8,0},{10,2},{12,4},{14,6},{16,24},{18,... | collective-permute-start | bytes 294920 | tf_op jit(solution)/shard_map/ppermute | solution.py:420
  97.5 26.6 %collective-permute-start.18 = (bf16[384,128]{1,0:T(8,128)(2,1)S(1)}, bf16[384,128]{1,0:T(8,128)(2,1)S(1)}, u32[]{:S(2)}, u32[]{:S(2)}) collective-permute-start(bf16[384,128]{1,0:T(8,128)(2,1)S(1)} %get-tuple-element.125), channel_id=1, source_target_pairs={{0,10},{2,12},{4,14},{6,0},{8,2},{10,4},{12,6},{14,8},{16,26},{18,... | collective-permute-start | bytes 294920 | tf_op jit(solution)/shard_map/ppermute | solution.py:420
  111.2 12.9 %collective-permute-start.19 = (bf16[384,128]{1,0:T(8,128)(2,1)S(1)}, bf16[384,128]{1,0:T(8,128)(2,1)S(1)}, u32[]{:S(2)}, u32[]{:S(2)}) collective-permute-start(bf16[384,128]{1,0:T(8,128)(2,1)S(1)} %get-tuple-element.126), channel_id=1, source_target_pairs={{0,12},{2,14},{4,0},{6,2},{8,4},{10,6},{12,8},{14,10},{16,28},{18,... | collective-permute-start | bytes 294920 | tf_op jit(solution)/shard_map/ppermute | solution.py:420
  112.1 13.2 %collective-permute-start.20 = (bf16[384,128]{1,0:T(8,128)(2,1)S(1)}, bf16[384,128]{1,0:T(8,128)(2,1)S(1)}, u32[]{:S(2)}, u32[]{:S(2)}) collective-permute-start(bf16[384,128]{1,0:T(8,128)(2,1)S(1)} %get-tuple-element.127), channel_id=1, source_target_pairs={{0,14},{2,0},{4,2},{6,4},{8,6},{10,8},{12,10},{14,12},{16,30},{18,... | collective-permute-start | bytes 294920 | tf_op jit(solution)/shard_map/ppermute | solution.py:420
  125.4 0.6 copy-start.2
  126.0 36.9 %copy-start = (bf16[384,2048]{1,0:T(8,128)(2,1)S(1)}, bf16[384,2048]{1,0:T(8,128)(2,1)}, u32[]{:S(2)}) copy-start(bf16[384,2048]{1,0:T(8,128)(2,1)} %q_ref.3) | copy-start | bytes 4718596
  126.0 36.9 %copy-start.3 = (bf16[384,128]{1,0:T(8,128)(2,1)S(1)}, bf16[384,128]{1,0:T(8,128)(2,1)}, u32[]{:S(2)}) copy-start(bf16[384,128]{1,0:T(8,128)(2,1)} %copy-done.2) | copy-start | bytes 294916
  143.6 12.2 %collective-permute-start.21 = (bf16[384,128]{1,0:T(8,128)(2,1)S(1)}, bf16[384,128]{1,0:T(8,128)(2,1)S(1)}, u32[]{:S(2)}, u32[]{:S(2)}) collective-permute-start(bf16[384,128]{1,0:T(8,128)(2,1)S(1)} %get-tuple-element.129), channel_id=1, source_target_pairs={{0,2},{2,4},{4,6},{6,8},{8,10},{10,12},{12,14},{14,0},{16,18},{18,... | collective-permute-start | bytes 294920 | tf_op jit(solution)/shard_map/ppermute | solution.py:420
  144.6 12.9 %collective-permute-start.22 = (bf16[384,128]{1,0:T(8,128)(2,1)S(1)}, bf16[384,128]{1,0:T(8,128)(2,1)S(1)}, u32[]{:S(2)}, u32[]{:S(2)}) collective-permute-start(bf16[384,128]{1,0:T(8,128)(2,1)S(1)} %get-tuple-element.130), channel_id=1, source_target_pairs={{0,4},{2,6},{4,8},{6,10},{8,12},{10,14},{12,0},{14,2},{16,20},{18,... | collective-permute-start | bytes 294920 | tf_op jit(solution)/shard_map/ppermute | solution.py:420
  149.5 10.9 %collective-permute-start.23 = (bf16[384,128]{1,0:T(8,128)(2,1)S(1)}, bf16[384,128]{1,0:T(8,128)(2,1)S(1)}, u32[]{:S(2)}, u32[]{:S(2)}) collective-permute-start(bf16[384,128]{1,0:T(8,128)(2,1)S(1)} %get-tuple-element.131), channel_id=1, source_target_pairs={{0,6},{2,8},{4,10},{6,12},{8,14},{10,0},{12,2},{14,4},{16,22},{18,... | collective-permute-start | bytes 294920 | tf_op jit(solution)/shard_map/ppermute | solution.py:420
  154.6 5.8 %collective-permute-start.24 = (bf16[384,128]{1,0:T(8,128)(2,1)S(1)}, bf16[384,128]{1,0:T(8,128)(2,1)S(1)}, u32[]{:S(2)}, u32[]{:S(2)}) collective-permute-start(bf16[384,128]{1,0:T(8,128)(2,1)S(1)} %get-tuple-element.132), channel_id=1, source_target_pairs={{0,8},{2,10},{4,12},{6,14},{8,0},{10,2},{12,4},{14,6},{16,24},{18,... | collective-permute-start | bytes 294920 | tf_op jit(solution)/shard_map/ppermute | solution.py:420
  154.6 5.8 %collective-permute-start.25 = (bf16[384,128]{1,0:T(8,128)(2,1)S(1)}, bf16[384,128]{1,0:T(8,128)(2,1)S(1)}, u32[]{:S(2)}, u32[]{:S(2)}) collective-permute-start(bf16[384,128]{1,0:T(8,128)(2,1)S(1)} %get-tuple-element.133), channel_id=1, source_target_pairs={{0,10},{2,12},{4,14},{6,0},{8,2},{10,4},{12,6},{14,8},{16,26},{18,... | collective-permute-start | bytes 294920 | tf_op jit(solution)/shard_map/ppermute | solution.py:420
  155.8 6.1 %collective-permute-start.26 = (bf16[384,128]{1,0:T(8,128)(2,1)S(1)}, bf16[384,128]{1,0:T(8,128)(2,1)S(1)}, u32[]{:S(2)}, u32[]{:S(2)}) collective-permute-start(bf16[384,128]{1,0:T(8,128)(2,1)S(1)} %get-tuple-element.134), channel_id=1, source_target_pairs={{0,12},{2,14},{4,0},{6,2},{8,4},{10,6},{12,8},{14,10},{16,28},{18,... | collective-permute-start | bytes 294920 | tf_op jit(solution)/shard_map/ppermute | solution.py:420
  157.4 5.5 %collective-permute-start.27 = (bf16[384,128]{1,0:T(8,128)(2,1)S(1)}, bf16[384,128]{1,0:T(8,128)(2,1)S(1)}, u32[]{:S(2)}, u32[]{:S(2)}) collective-permute-start(bf16[384,128]{1,0:T(8,128)(2,1)S(1)} %get-tuple-element.135), channel_id=1, source_target_pairs={{0,14},{2,0},{4,2},{6,4},{8,6},{10,8},{12,10},{14,12},{16,30},{18,... | collective-permute-start | bytes 294920 | tf_op jit(solution)/shard_map/ppermute | solution.py:420
